TPU v7x, 512 devices: a whole 4x4x16 slice. The times are simulated.
512 devices in a mesh: gx: 8 (over y_hi, x), gy: 16 (over z), gz: 4 (over y_lo, core).
Axes of the slice: x: 4, y: 4 (y_hi: 2, y_lo: 2; y = y_hi * 2 + y_lo), z: 16, core: 2. Of those that a mesh axis runs over, the one named last changes fastest.
Arguments:
- rhs_fine: float32 [16, 32, 8, 2048], P('gx', 'gy', 'gz'), may hold values from -6 to 6
- fine_blocks: float32 [16, 32, 8, 7, 4096], P('gx', 'gy', 'gz'), may hold values from -2.5 to 2.5
- fine_links: int32 [16, 32, 8, 6], P('gx', 'gy', 'gz'), may hold values 0 or 1
- fine_smoother: float32 [16, 32, 8, 4096], P('gx', 'gy', 'gz'), may hold values from -2 to 2
- fine_prolong: float32 [16, 32, 8, 4096], P('gx', 'gy', 'gz'), may hold values from -0.75 to 0.75
- mid_blocks: float32 [8, 16, 4, 7, 4096], P('gx', 'gy'), may hold values from -2.5 to 2.5
- mid_links: int32 [8, 16, 4, 6], P('gx', 'gy'), may hold values 0 or 1
- mid_smoother: float32 [8, 16, 4, 4096], P('gx', 'gy'), may hold values from -2 to 2
- mid_prolong: float32 [8, 16, 4, 4096], P('gx', 'gy'), may hold values from -0.75 to 0.75
- coarse_blocks: float32 [8, 8, 2, 7, 4096], P('gx'), may hold values from -2.5 to 2.5
- coarse_links: int32 [8, 8, 2, 6], P('gx'), may hold values 0 or 1
- coarse_smoother: float32 [8, 8, 2, 4096], P('gx'), may hold values from -2 to 2
- lower_bounds: float32 [3], replicated, may hold values from 0.08 to 0.3
- upper_bounds: float32 [3], replicated, may hold values from 1.6 to 2.6
Outputs:
- solution: float32 [16, 32, 8, 2048], P('gx', 'gy', 'gz')
- residual: float32 [16, 32, 8, 2048], P('gx', 'gy', 'gz')
All inputs are finite; a program needn't handle non-finite values. No bound on the sum of `fine_links` or of `mid_links` or of `coarse_links` on one device may be relied on, other than what follows from the above.
Results may differ from a plain program's by a relative error of at most 0.0003.
Values sent between devices are 32-bit elements; how exact they have to be, the bound alone decides.
A program may use at most 128 MiB of HBM per device.

v0:
```python
import jax
import jax.numpy as jnp
from jax import lax
from jax.experimental import pallas as pl
from jax.experimental.pallas import tpu as pltpu
from jax.sharding import PartitionSpec as P

F32 = jnp.float32
BF16 = jnp.bfloat16
MESH = pl.DeviceIdType.MESH


def lane(shape=(64, 128)):
    return lax.broadcasted_iota(jnp.int32, shape, 1)


def low(shape=(64, 128)):
    return lane(shape) < 64


def pick(group, parts):
    return jnp.where(
        group < 2,
        jnp.where(group == 0, parts[0], parts[1]),
        jnp.where(group == 2, parts[2], parts[3]),
    )


def roll(x, shift):
    return pltpu.roll(x, shift, 1) if shift else x


def split(v):
    high = v.astype(BF16)
    return high, (v - high.astype(F32)).astype(BF16)


def wide(v):
    return jnp.concatenate(split(v), axis=1)


def tall(v):
    high, rest = split(v)
    return jnp.concatenate([high, rest, high, rest], axis=0)


def matmul(left, right):
    return jnp.dot(left, right, preferred_element_type=F32)


def rows_of(ref, node, many):
    return ref[pl.ds(node, 32, stride=many), :]


def weave(ref, left, right):
    first = low((32, 128))
    left_turned, right_turned = roll(left, 64), roll(right, 64)
    ref[pl.ds(0, 32, stride=2), :] = jnp.where(first, left, right_turned)
    ref[pl.ds(1, 32, stride=2), :] = jnp.where(first, left_turned, right)
    return ref[...]


def double(block):
    high, rest = split(block)
    return jnp.concatenate([high, rest], axis=1)


def fold_fine(product, group):
    total = (product[:256, :128] + product[:256, 128:]) + (
        product[256:, :128] + product[256:, 128:]
    )
    return pick(group, [total[64 * g : 64 * g + 64] for g in range(4)])


def kernel(
    rhs_hbm,
    fblocks_hbm,
    flinks,
    fsmooth_hbm,
    fprolong_hbm,
    mblocks_hbm,
    mlinks,
    msmooth_hbm,
    mprolong_hbm,
    cblocks_hbm,
    clinks,
    csmooth_hbm,
    lowers,
    uppers,
    solution_ref,
    residual_ref,
    rhs_raw,
    fblocks,
    fsmooth,
    fprolong,
    mblocks,
    msmooth,
    mprolong,
    cblocks,
    csmooth,
    in_sems,
    packed,
    woven,
    inner_l,
    outer_l,
    smooth_l,
    prolong_l,
    restrict_l,
    one_outer,
    one_centre,
    one_smooth,
    one_prolong,
    face_send,
    face_pack,
    face_recv,
    node_send,
    node_recv,
    sib_send,
    sib_recv,
    face_out_sem,
    face_in_sem,
    node_out_sem,
    node_in_sem,
    sib_out_sem,
    sib_in_sem,
):
    size = {name: lax.axis_size(name) for name in ("gx", "gy", "gz")}
    at = {name: lax.axis_index(name) for name in ("gx", "gy", "gz")}

    def beside(name, step):
        return {name: lax.rem(at[name] + (step + size[name]), size[name])}

    mate_y = at["gy"] + 1 - 2 * lax.rem(at["gy"], 2)
    mate_z = at["gz"] + 1 - 2 * lax.rem(at["gz"], 2)
    near = [
        beside("gx", -1),
        beside("gx", 1),
        beside("gy", -1),
        beside("gy", 1),
        beside("gz", -1),
        beside("gz", 1),
    ]
    coarse_near = [
        beside("gx", -1),
        beside("gx", 1),
        beside("gy", -2),
        beside("gy", 2),
        beside("gz", 2),
    ]
    siblings = [{"gy": mate_y}, {"gz": mate_z}, {"gy": mate_y, "gz": mate_z}]
    parent_y = lax.div(at["gy"], 2)
    parent_z = lax.div(at["gz"], 2)

    loads = [
        pltpu.make_async_copy(src, dst, in_sems.at[i])
        for i, (src, dst) in enumerate(
            [
                (rhs_hbm, rhs_raw),
                (fsmooth_hbm, fsmooth),
                (fblocks_hbm, fblocks),
                (fprolong_hbm, fprolong),
                (mblocks_hbm, mblocks),
                (msmooth_hbm, msmooth),
                (mprolong_hbm, mprolong),
                (cblocks_hbm.at[parent_y], cblocks),
                (csmooth_hbm.at[parent_y], csmooth),
            ]
        )
    ]
    for load in loads:
        load.start()

    barrier = pltpu.get_barrier_semaphore()
    greeted = near + coarse_near[2:] + siblings[2:]
    for device in greeted:
        pl.semaphore_signal(barrier, inc=1, device_id=device, device_id_type=MESH)

    def has(name, step):
        if step < 0:
            return jnp.where(at[name] >= -step, 1.0, 0.0).astype(F32)
        return jnp.where(at[name] < size[name] - step, 1.0, 0.0).astype(F32)

    reach = [has("gx", -1), has("gx", 1), has("gy", -1), has("gy", 1), has("gz", -1), has("gz", 1)]
    coarse_reach = [has("gx", -1), has("gx", 1), has("gy", -2), has("gy", 2), has("gz", -2), has("gz", 2)]

    group = lax.shift_right_logical(lane(), 5)
    group16 = lax.shift_right_logical(lane((16, 128)), 5)
    first_half = low()
    even = lax.rem(group, 2) == 0

    def coefficients(level):
        upper = jnp.full((1, 128), uppers[level], F32)
        lower = jnp.full((1, 128), lowers[level], F32)
        theta = (upper + lower) * 0.5
        delta = (upper - lower) * 0.5
        sigma = theta / delta
        rho = 1.0 / sigma
        steps = []
        for _ in range(3 if level == 2 else 1):
            later = 1.0 / (2.0 * sigma - rho)
            steps.append((later * rho, 2.0 * later / delta))
            rho = later
        return 1.0 / theta, steps

    def from_natural(raw, out):
        for a in range(2):
            nodes = [raw[a, g // 2, pl.ds(g % 2, 16, stride=2), :] for g in range(4)]
            for q in range(4):
                out[a, pl.ds(q, 16, stride=4), :] = pick(
                    group16, [roll(nodes[g], 32 * ((g - q) % 4)) for g in range(4)]
                )

    def to_natural(field, out):
        for a in range(2):
            packed[a] = field[a]
        for a in range(2):
            rows = [packed[a, pl.ds(q, 16, stride=4), :] for q in range(4)]
            for g in range(4):
                out[a, g // 2, pl.ds(g % 2, 16, stride=2), :] = pick(
                    group16, [roll(rows[q], 32 * ((q - g) % 4)) for q in range(4)]
                )

    def each(times, body):
        def step(n, carry):
            body(n)
            return carry

        lax.fori_loop(0, times, step, 0)

    def put(ref, a, g, column, value, rest_at=256):
        high, rest = split(value)
        rows = pl.ds(pl.multiple_of(g * 64, 64), 64)
        rest_rows = pl.ds(pl.multiple_of(rest_at + g * 64, 64), 64)
        ref[a, rows, column : column + 128] = high
        ref[a, rest_rows, column : column + 128] = rest

    def double_fine(raw, out, slot, turned=None):
        for a in range(2):
            for b in range(2):
                both = []
                for c in range(2):
                    g = 2 * b + c
                    block = rows_of(raw.at[a, b], c, 2)
                    block = weave(woven.at[slot + 4 * a + g], block, block)
                    out[a, 64 * g : 64 * g + 64, :] = double(block)
                    both.append(block)
                if turned is not None:
                    column = 128 * (2 * a + b)
                    high, rest = split(jnp.transpose(jnp.concatenate(both, axis=0))[0:64, :])
                    turned[0:64, column : column + 128] = high
                    turned[64:128, column : column + 128] = rest

    def prepare_fine():
        def body(n):
            a, b = lax.div(n, 2), lax.rem(n, 2)

            def far(axis, here):
                return jnp.where(here == 0, reach[2 * axis], reach[2 * axis + 1])

            for c in range(2):
                g = 2 * b + c

                def block(d, far=None):
                    flag = flinks[a, b, c, d - 1].astype(F32)
                    if far is not None:
                        flag = flag * far
                    return rows_of(fblocks.at[a, b, d], c, 2) * flag

                slots = woven.at[pl.ds(n * 8 + c * 4, 4)]
                centre = rows_of(fblocks.at[a, b, 0], c, 2)
                put(inner_l, a, g, 0, weave(slots.at[0], centre, block(2 - a)))
                put(inner_l, a, g, 128, weave(slots.at[1], block(4 - b), block(6 - c)))
                put(outer_l, a, g, 0, weave(slots.at[2], block(1 + a, far(0, a)), block(3 + b, far(1, b))))
                last = block(5 + c, far(2, c))
                put(outer_l, a, g, 128, weave(slots.at[3], last, jnp.zeros_like(last)))

        each(4, body)

    def one_block(raw, row, many, out, slot):
        block = rows_of(raw, row, many)
        block = weave(woven.at[slot], block, block)
        out[...] = double(block)
        return block

    def one_turned(block, out):
        out[...] = double(jnp.transpose(jnp.concatenate([block, block], axis=0))[0:64, :])

    def one_operator(raw, row, many, flag, level, slot):
        one_block(raw.at[0], row, many, one_centre.at[level], slot)
        for pair in range(3):
            d = 2 * pair + 1
            put(
                one_outer,
                level,
                0,
                128 * pair,
                weave(
                    woven.at[slot + 1 + pair],
                    rows_of(raw.at[d], row, many) * flag(d),
                    rows_of(raw.at[d + 1], row, many) * flag(d + 1),
                ),
                64,
            )

    def faces(slot):
        copies = []
        for side in range(6):
            if side == 0:
                src, dst = face_send.at[slot, 0], 1
            elif side == 1:
                src, dst = face_send.at[slot, 1], 0
            else:
                src, dst = face_pack.at[slot, side - 2], side ^ 1
            copies.append(
                pltpu.make_async_remote_copy(
                    src_ref=src,
                    dst_ref=face_recv.at[slot, dst],
                    send_sem=face_out_sem.at[slot, side],
                    recv_sem=face_in_sem.at[slot, dst],
                    device_id=near[side],
                    device_id_type=MESH,
                )
            )
        return copies

    def send_faces(slot, field):
        copies = faces(slot)
        zero, one = field
        face_send[slot, 0] = zero
        face_send[slot, 1] = one
        copies[0].start()
        copies[1].start()
        face_pack[slot, 0] = jnp.where(first_half, zero, roll(one, 64))
        copies[2].start()
        face_pack[slot, 1] = jnp.where(first_half, roll(zero, 64), one)
        copies[3].start()
        face_pack[slot, 2] = jnp.where(even, zero, roll(one, 32))
        copies[4].start()
        face_pack[slot, 3] = jnp.where(even, roll(zero, 96), one)
        copies[5].start()

    def wait_faces(slot):
        for copy in faces(slot):
            copy.wait_recv()

    def nodes(slot, devices, far_side):
        return [
            pltpu.make_async_remote_copy(
                src_ref=node_send.at[slot],
                dst_ref=node_recv.at[slot, far_side[side]],
                send_sem=node_out_sem.at[slot, side],
                recv_sem=node_in_sem.at[slot, far_side[side]],
                device_id=device,
                device_id_type=MESH,
            )
            for side, device in enumerate(devices)
        ]

    def middle_copies(slot):
        return nodes(slot, near, [1, 0, 3, 2, 5, 4])

    def coarse_copies(slot):
        return nodes(slot, coarse_near, [1, 0, 3, 2, 4])

    def pack(v):
        return pick(
            group16, [roll(v[16 * q : 16 * q + 16], 32 * q) for q in range(4)]
        )

    def unpack(v):
        return jnp.concatenate([roll(v, (128 - 32 * q) % 128) for q in range(4)], axis=0)

    def sib_copies():
        return [
            pltpu.make_async_remote_copy(
                src_ref=sib_send,
                dst_ref=sib_recv.at[i],
                send_sem=sib_out_sem.at[i],
                recv_sem=sib_in_sem.at[i],
                device_id=device,
                device_id_type=MESH,
            )
            for i, device in enumerate(siblings)
        ]

    def by_node(left, right):
        out = []
        for a in range(2):
            product = matmul(left[a], right[a])
            out.append(pick(group, [product[64 * g : 64 * g + 64] for g in range(4)]))
        return out

    def smooth(field):
        return by_node(smooth_l, [tall(field[0]), tall(field[1])])

    def inner(field):
        out = []
        for a in range(2):
            own = field[a]
            turned_y = roll(own, 64)
            turned_z = jnp.where(even, roll(own, 96), roll(own, 32))
            right = jnp.concatenate(
                [wide(own), wide(field[1 - a]), wide(turned_y), wide(turned_z)], axis=0
            )
            out.append(fold_fine(matmul(inner_l[a], right), group))
        return out

    def outer(slot):
        near_y, far_y = face_recv[slot, 2], face_recv[slot, 3]
        near_z, far_z = face_recv[slot, 4], face_recv[slot, 5]
        along_y = [
            jnp.where(first_half, near_y, roll(far_y, 64)),
            jnp.where(first_half, roll(near_y, 64), far_y),
        ]
        along_z = [
            jnp.where(even, near_z, roll(far_z, 32)),
            jnp.where(even, roll(near_z, 96), far_z),
        ]
        out = []
        for a in range(2):
            z = wide(along_z[a])
            right = jnp.concatenate([wide(face_recv[slot, a]), wide(along_y[a]), z, z], axis=0)
            out.append(fold_fine(matmul(outer_l[a], right), group))
        return out

    def one_smoothed(level, v):
        return matmul(one_smooth[level], tall(v))

    def one_apply(level, copies, slot, v):
        total = matmul(one_centre[level], tall(v))
        for copy in copies:
            copy.wait_recv()
        parts = [wide(unpack(node_recv[slot, side])) for side in range(len(copies))]
        if len(parts) == 5:
            parts.append(parts[4])
        product = matmul(one_outer[level], jnp.concatenate(parts, axis=0))
        return total + (
            (product[0:64, 0:128] + product[0:64, 128:256])
            + (product[64:128, 0:128] + product[64:128, 128:256])
        )

    def send_node(slot, copies, v):
        node_send[slot] = pack(v)
        for copy in copies:
            copy.start()

    def plus(x, y):
        return [p + q for p, q in zip(x, y)]

    def minus(x, y):
        return [p - q for p, q in zip(x, y)]

    def scaled(x, factor):
        return [p * factor for p in x]

    inverse, steps = coefficients(0)
    loads[1].wait()
    double_fine(fsmooth, smooth_l, 32)
    loads[0].wait()
    from_natural(rhs_raw, packed)
    resid = [packed[0], packed[1]]
    first = scaled(smooth(resid), inverse)
    pl.semaphore_wait(barrier, len(greeted))
    send_faces(0, first)

    loads[2].wait()
    prepare_fine()
    resid = minus(resid, inner(first))
    wait_faces(0)
    resid = minus(resid, outer(0))
    keep, push = steps[0]
    second = plus(scaled(first, keep), scaled(smooth(resid), push))
    send_faces(1, second)
    fine_first = plus(first, second)

    loads[3].wait()
    double_fine(fprolong, prolong_l, 40, restrict_l)
    loads[5].wait()
    one_block(msmooth, at["gz"], 4, one_smooth.at[0], 48)
    loads[4].wait()
    one_operator(
        mblocks, at["gz"], 4, lambda d: mlinks[0, 0, at["gz"], d - 1].astype(F32) * reach[d - 1], 0, 50
    )

    resid = minus(resid, inner(second))
    wait_faces(1)
    resid = minus(resid, outer(1))

    parts = []
    for a in range(2):
        for g in range(4):
            parts.append(wide(roll(resid[a], (128 - 32 * g) % 128)))
    product = matmul(restrict_l[...], jnp.concatenate(parts, axis=0))
    mid_resid = (product[0:64, 0:128] + product[0:64, 128:256]) + (
        product[64:128, 0:128] + product[64:128, 128:256]
    )
    mid_inverse, mid_steps = coefficients(1)
    mid_keep, mid_push = mid_steps[0]
    first = one_smoothed(0, mid_resid) * mid_inverse
    copies = middle_copies(0)
    send_node(0, copies, first)
    loads[6].wait()
    one_turned(one_block(mprolong, at["gz"], 4, one_prolong.at[0], 49), one_prolong.at[1])
    mid_resid = mid_resid - one_apply(0, copies, 0, first)
    second = first * mid_keep + one_smoothed(0, mid_resid) * mid_push
    copies = middle_copies(1)
    send_node(1, copies, second)
    mid_field = first + second
    loads[8].wait()
    one_block(csmooth, parent_z, 2, one_smooth.at[1], 54)
    loads[7].wait()
    one_operator(
        cblocks,
        parent_z,
        2,
        lambda d: clinks[0, d - 1, parent_z, parent_y].astype(F32) * coarse_reach[d - 1],
        1,
        55,
    )
    mid_resid = mid_resid - one_apply(0, copies, 1, second)

    own = pack(matmul(one_prolong[1], tall(mid_resid)))
    sib_send[...] = own
    copies = sib_copies()
    for copy in copies:
        copy.start()
    coarse_inverse, coarse_steps = coefficients(2)
    for copy in copies:
        copy.wait_recv()
    coarse_resid = unpack((own + sib_recv[0]) + (sib_recv[1] + sib_recv[2]))
    step = one_smoothed(1, coarse_resid) * coarse_inverse
    coarse_field = step
    for sweep in range(3):
        copies = coarse_copies(2 + sweep)
        send_node(2 + sweep, copies, step)
        coarse_resid = coarse_resid - one_apply(1, copies, 2 + sweep, step)
        keep, push = coarse_steps[sweep]
        step = step * keep + one_smoothed(1, coarse_resid) * push
        coarse_field = coarse_field + step

    lifted = matmul(one_prolong[0], tall(coarse_field))
    copies = middle_copies(5)
    send_node(5, copies, lifted)
    mid_field = mid_field + lifted
    mid_resid = mid_resid - one_apply(0, copies, 5, lifted)
    first = one_smoothed(0, mid_resid) * mid_inverse
    copies = middle_copies(6)
    send_node(6, copies, first)
    mid_field = mid_field + first
    mid_resid = mid_resid - one_apply(0, copies, 6, first)
    mid_field = mid_field + (first * mid_keep + one_smoothed(0, mid_resid) * mid_push)

    inverse, steps = coefficients(0)
    keep, push = steps[0]
    alone = jnp.where(group == 0, mid_field, 0.0)
    alone = alone + roll(alone, 32)
    alone = tall(alone + roll(alone, 64))
    lifted = by_node(prolong_l, [alone, alone])
    send_faces(2, lifted)
    fine_field = plus(fine_first, lifted)
    resid = minus(resid, inner(lifted))
    wait_faces(2)
    resid = minus(resid, outer(2))
    first = scaled(smooth(resid), inverse)
    send_faces(3, first)
    fine_field = plus(fine_field, first)
    resid = minus(resid, inner(first))
    wait_faces(3)
    resid = minus(resid, outer(3))
    second = plus(scaled(first, keep), scaled(smooth(resid), push))
    send_faces(4, second)
    fine_field = plus(fine_field, second)
    to_natural(fine_field, solution_ref)
    resid = minus(resid, inner(second))
    wait_faces(4)
    resid = minus(resid, outer(4))
    to_natural(resid, residual_ref)

    for slot in range(5):
        for copy in faces(slot):
            copy.wait_send()
    for slot in (0, 1, 5, 6):
        for copy in middle_copies(slot):
            copy.wait_send()
    for slot in (2, 3, 4):
        for copy in coarse_copies(slot):
            copy.wait_send()
    for copy in sib_copies():
        copy.wait_send()


def interleaved(x):
    nodes, n = x.shape[-2:]
    x = jnp.swapaxes(x.reshape(x.shape[:-1] + (n // 128, 128)), -3, -2)
    return x.reshape(x.shape[:-3] + (n // 128 * nodes, 128))


def by_link(x):
    return interleaved(jnp.swapaxes(x, -3, -2))


def body(*args):
    (rhs, fblocks, flinks, fsmooth, fprolong, mblocks, mlinks, msmooth, mprolong) = args[:9]
    (cblocks, clinks, csmooth, lowers, uppers) = args[9:]
    shape = rhs.shape
    rhs, fsmooth, fprolong = interleaved(rhs), interleaved(fsmooth), interleaved(fprolong)
    fblocks, mblocks, cblocks = by_link(fblocks), by_link(mblocks)[0, 0], by_link(cblocks)[0]
    msmooth, mprolong = interleaved(msmooth)[0, 0], interleaved(mprolong)[0, 0]
    csmooth = interleaved(csmooth)[0]
    clinks = jnp.transpose(clinks, (0, 3, 2, 1))
    anywhere = pl.BlockSpec(memory_space=pl.ANY)
    scalars = pl.BlockSpec(memory_space=pltpu.SMEM)
    vmem = pl.BlockSpec(memory_space=pltpu.VMEM)
    dma = pltpu.SemaphoreType.DMA
    outs = pl.pallas_call(
        kernel,
        out_shape=(
            jax.ShapeDtypeStruct(rhs.shape, F32),
            jax.ShapeDtypeStruct(rhs.shape, F32),
        ),
        in_specs=[
            anywhere,
            anywhere,
            scalars,
            anywhere,
            anywhere,
            anywhere,
            scalars,
            anywhere,
            anywhere,
            anywhere,
            scalars,
            anywhere,
            scalars,
            scalars,
        ],
        out_specs=(vmem, vmem),
        scratch_shapes=[
            pltpu.VMEM(rhs.shape, F32),
            pltpu.VMEM(fblocks.shape, F32),
            pltpu.VMEM(fsmooth.shape, F32),
            pltpu.VMEM(fprolong.shape, F32),
            pltpu.VMEM(mblocks.shape, F32),
            pltpu.VMEM(msmooth.shape, F32),
            pltpu.VMEM(mprolong.shape, F32),
            pltpu.VMEM(cblocks.shape[1:], F32),
            pltpu.VMEM(csmooth.shape[1:], F32),
            dma((9,)),
            pltpu.VMEM((2, 64, 128), F32),
            pltpu.VMEM((59, 64, 128), F32),
            pltpu.VMEM((2, 512, 256), BF16),
            pltpu.VMEM((2, 512, 256), BF16),
            pltpu.VMEM((2, 256, 256), BF16),
            pltpu.VMEM((2, 256, 256), BF16),
            pltpu.VMEM((128, 512), BF16),
            pltpu.VMEM((2, 128, 384), BF16),
            pltpu.VMEM((2, 64, 256), BF16),
            pltpu.VMEM((2, 64, 256), BF16),
            pltpu.VMEM((2, 64, 256), BF16),
            pltpu.VMEM((5, 2, 64, 128), F32),
            pltpu.VMEM((5, 4, 64, 128), F32),
            pltpu.VMEM((5, 6, 64, 128), F32),
            pltpu.VMEM((7, 16, 128), F32),
            pltpu.VMEM((7, 6, 16, 128), F32),
            pltpu.VMEM((16, 128), F32),
            pltpu.VMEM((3, 16, 128), F32),
            dma((5, 6)),
            dma((5, 6)),
            dma((7, 6)),
            dma((7, 6)),
            dma((3,)),
            dma((3,)),
        ],
        compiler_params=pltpu.CompilerParams(
            collective_id=0, has_side_effects=True, vmem_limit_bytes=56 * 1024 * 1024
        ),
    )(
        rhs,
        fblocks,
        flinks,
        fsmooth,
        fprolong,
        mblocks,
        mlinks,
        msmooth,
        mprolong,
        cblocks,
        clinks,
        csmooth,
        lowers,
        uppers,
    )
    return tuple(
        jnp.swapaxes(out.reshape(2, 2, 16, 2, 128), 2, 3).reshape(shape) for out in outs
    )


def solution(mesh):
    return jax.shard_map(
        body,
        mesh=mesh,
        in_specs=(
            P("gx", "gy", "gz", None),
            P("gx", "gy", "gz", None, None),
            P("gx", "gy", "gz", None),
            P("gx", "gy", "gz", None),
            P("gx", "gy", "gz", None),
            P("gx", "gy", None, None, None),
            P("gx", "gy", None, None),
            P("gx", "gy", None, None),
            P("gx", "gy", None, None),
            P("gx", None, None, None, None),
            P("gx", None, None, None),
            P("gx", None, None, None),
            P(),
            P(),
        ),
        out_specs=(P("gx", "gy", "gz", None), P("gx", "gy", "gz", None)),
        check_vma=False,
    )
```

profile of v0, /device:TPU:1, one launch (start us, length us, event | category | flops | bytes accessed | tf_op | source)
XLA Modules:
  0.0 84.0 jit_solution(17306215584784096642)
XLA Ops:
  0.6 80.4 %shard_map.149 = (f32[2,2,32,128]{3,2,1,0:T(8,128)}, f32[2,2,32,128]{3,2,1,0:T(8,128)}) custom-call(f32[2,2,32,128]{3,2,1,0:T(8,128)} %bitcast.68, f32[2,2,7,64,128]{4,3,2,1,0:T(8,128)} %bitcast.63, s32[2,2,2,6]{3,2,1,0:T(2,128)} %flinks.1, f32[2,2,64,128]{3,2,1,0:T(8,128)} %bitcast.66, f32[2,2,64,128]{3,2,1,0:T(8,128)} %bitcast.67, ...), custom_call_target="tpu_custom_call" | custom-call | tf_op jit(solution)/shard_map/pallas_call | solution.py:615
  81.0 1.5 %copy.29 = f32[2,2,2,2048]{3,2,1,0:T(2,128)} copy(f32[2,2,2,2048]{3,2,1,0:T(2,128)} %bitcast.72) | data formatting | bytes 131072
  82.5 1.5 %copy.30 = f32[2,2,2,2048]{3,2,1,0:T(2,128)} copy(f32[2,2,2,2048]{3,2,1,0:T(2,128)} %bitcast.71) | data formatting | bytes 131072
where the time goes:
time: 84.3 us; the launch traced here: 84 us
  Pallas kernels  80.4 us (95%)
  local copies, waits for them, and re-layouts  2.95 us (3%)
    pallas_call x1, Pallas kernels, body(): pl.pallas_call(kernel, out_shape=(jax.ShapeDtypeStruct(rhs.shape, F32), j...  80.4 us
    unnamed x2, local copies, waits for them, and re-layouts  2.95 us

commit v1 on v0

--- a/solution.py
+++ b/solution.py
@@ -75,20 +75,25 @@
 def kernel(
     rhs_hbm,
     fblocks_hbm,
-    flinks,
+    flinks_hbm,
     fsmooth_hbm,
     fprolong_hbm,
     mblocks_hbm,
-    mlinks,
+    mlinks_hbm,
     msmooth_hbm,
     mprolong_hbm,
     cblocks_hbm,
+    clinks_hbm,
+    csmooth_hbm,
+    lowers_hbm,
+    uppers_hbm,
+    solution_ref,
+    residual_ref,
+    flinks,
+    mlinks,
     clinks,
-    csmooth_hbm,
     lowers,
     uppers,
-    solution_ref,
-    residual_ref,
     rhs_raw,
     fblocks,
     fsmooth,
@@ -115,14 +120,19 @@
     face_recv,
     node_send,
     node_recv,
-    sib_send,
-    sib_recv,
+    term_send,
+    term_recv,
+    block_send,
+    block_recv,
+    near_smooth,
     face_out_sem,
     face_in_sem,
     node_out_sem,
     node_in_sem,
-    sib_out_sem,
-    sib_in_sem,
+    term_out_sem,
+    term_in_sem,
+    block_out_sem,
+    block_in_sem,
 ):
     size = {name: lax.axis_size(name) for name in ("gx", "gy", "gz")}
     at = {name: lax.axis_index(name) for name in ("gx", "gy", "gz")}
@@ -147,33 +157,55 @@
         beside("gy", 2),
         beside("gz", 2),
     ]
-    siblings = [{"gy": mate_y}, {"gz": mate_z}, {"gy": mate_y, "gz": mate_z}]
+
+    def four(shift):
+        name, step = shift
+        place = dict(at)
+        mates = {"gy": mate_y, "gz": mate_z}
+        if name is not None:
+            place[name] = lax.rem(at[name] + (step + size[name]), size[name])
+        if name in mates:
+            mates[name] = lax.rem(mates[name] + (step + size[name]), size[name])
+        return [
+            place,
+            {**place, "gy": mates["gy"]},
+            {**place, "gz": mates["gz"]},
+            {**place, **mates},
+        ]
+
+    shifts = [(None, 0), ("gx", -1), ("gx", 1), ("gy", -2), ("gy", 2), ("gz", 2)]
+    across = [0, 2, 1, 4, 3, 5]
+    holders = [(m, e, device) for m in range(6) for e, device in enumerate(four(shifts[m]))][1:]
     parent_y = lax.div(at["gy"], 2)
     parent_z = lax.div(at["gz"], 2)
+
+    barrier = pltpu.get_barrier_semaphore()
+    for _, _, device in holders:
+        pl.semaphore_signal(barrier, inc=1, device_id=device, device_id_type=MESH)
 
     loads = [
         pltpu.make_async_copy(src, dst, in_sems.at[i])
         for i, (src, dst) in enumerate(
             [
+                (fsmooth_hbm, fsmooth),
                 (rhs_hbm, rhs_raw),
-                (fsmooth_hbm, fsmooth),
+                (lowers_hbm, lowers),
+                (uppers_hbm, uppers),
+                (flinks_hbm, flinks),
                 (fblocks_hbm, fblocks),
                 (fprolong_hbm, fprolong),
+                (msmooth_hbm, msmooth),
+                (mlinks_hbm, mlinks),
                 (mblocks_hbm, mblocks),
-                (msmooth_hbm, msmooth),
                 (mprolong_hbm, mprolong),
+                (csmooth_hbm, csmooth),
+                (clinks_hbm, clinks),
                 (cblocks_hbm.at[parent_y], cblocks),
-                (csmooth_hbm.at[parent_y], csmooth),
             ]
         )
     ]
     for load in loads:
         load.start()
-
-    barrier = pltpu.get_barrier_semaphore()
-    greeted = near + coarse_near[2:] + siblings[2:]
-    for device in greeted:
-        pl.semaphore_signal(barrier, inc=1, device_id=device, device_id_type=MESH)
 
     def has(name, step):
         if step < 0:
@@ -370,17 +402,30 @@
     def unpack(v):
         return jnp.concatenate([roll(v, (128 - 32 * q) % 128) for q in range(4)], axis=0)
 
-    def sib_copies():
+    def term_copies():
         return [
             pltpu.make_async_remote_copy(
-                src_ref=sib_send,
-                dst_ref=sib_recv.at[i],
-                send_sem=sib_out_sem.at[i],
-                recv_sem=sib_in_sem.at[i],
+                src_ref=term_send,
+                dst_ref=term_recv.at[4 * across[m] + e],
+                send_sem=term_out_sem.at[4 * m + e],
+                recv_sem=term_in_sem.at[4 * across[m] + e],
                 device_id=device,
                 device_id_type=MESH,
             )
-            for i, device in enumerate(siblings)
+            for m, e, device in holders
+        ]
+
+    def block_copies():
+        return [
+            pltpu.make_async_remote_copy(
+                src_ref=block_send,
+                dst_ref=block_recv.at[1 - side],
+                send_sem=block_out_sem.at[side],
+                recv_sem=block_in_sem.at[1 - side],
+                device_id=near[side],
+                device_id_type=MESH,
+            )
+            for side in range(2)
         ]
 
     def by_node(left, right):
@@ -426,18 +471,20 @@
     def one_smoothed(level, v):
         return matmul(one_smooth[level], tall(v))
 
+    def one_outside(level, parts):
+        if len(parts) == 5:
+            parts = parts + [parts[4]]
+        product = matmul(one_outer[level], jnp.concatenate(parts, axis=0))
+        return (product[0:64, 0:128] + product[0:64, 128:256]) + (
+            product[64:128, 0:128] + product[64:128, 128:256]
+        )
+
     def one_apply(level, copies, slot, v):
         total = matmul(one_centre[level], tall(v))
         for copy in copies:
             copy.wait_recv()
         parts = [wide(unpack(node_recv[slot, side])) for side in range(len(copies))]
-        if len(parts) == 5:
-            parts.append(parts[4])
-        product = matmul(one_outer[level], jnp.concatenate(parts, axis=0))
-        return total + (
-            (product[0:64, 0:128] + product[0:64, 128:256])
-            + (product[64:128, 0:128] + product[64:128, 128:256])
-        )
+        return total + one_outside(level, parts)
 
     def send_node(slot, copies, v):
         node_send[slot] = pack(v)
@@ -453,18 +500,25 @@
     def scaled(x, factor):
         return [p * factor for p in x]
 
+    loads[0].wait()
+    double_fine(fsmooth, smooth_l, 32)
+    loads[1].wait()
+    from_natural(rhs_raw, packed)
+    loads[2].wait()
+    loads[3].wait()
     inverse, steps = coefficients(0)
-    loads[1].wait()
-    double_fine(fsmooth, smooth_l, 32)
-    loads[0].wait()
-    from_natural(rhs_raw, packed)
     resid = [packed[0], packed[1]]
     first = scaled(smooth(resid), inverse)
-    pl.semaphore_wait(barrier, len(greeted))
+    pl.semaphore_wait(barrier, len(holders))
     send_faces(0, first)
 
-    loads[2].wait()
+    loads[4].wait()
+    loads[5].wait()
     prepare_fine()
+    loads[11].wait()
+    block_send[...] = rows_of(csmooth.at[parent_y], parent_z, 2)
+    for copy in block_copies():
+        copy.start()
     resid = minus(resid, inner(first))
     wait_faces(0)
     resid = minus(resid, outer(0))
@@ -473,11 +527,12 @@
     send_faces(1, second)
     fine_first = plus(first, second)
 
-    loads[3].wait()
+    loads[6].wait()
     double_fine(fprolong, prolong_l, 40, restrict_l)
-    loads[5].wait()
+    loads[7].wait()
     one_block(msmooth, at["gz"], 4, one_smooth.at[0], 48)
-    loads[4].wait()
+    loads[8].wait()
+    loads[9].wait()
     one_operator(
         mblocks, at["gz"], 4, lambda d: mlinks[0, 0, at["gz"], d - 1].astype(F32) * reach[d - 1], 0, 50
     )
@@ -499,16 +554,26 @@
     first = one_smoothed(0, mid_resid) * mid_inverse
     copies = middle_copies(0)
     send_node(0, copies, first)
-    loads[6].wait()
+    loads[10].wait()
     one_turned(one_block(mprolong, at["gz"], 4, one_prolong.at[0], 49), one_prolong.at[1])
     mid_resid = mid_resid - one_apply(0, copies, 0, first)
     second = first * mid_keep + one_smoothed(0, mid_resid) * mid_push
     copies = middle_copies(1)
     send_node(1, copies, second)
     mid_field = first + second
-    loads[8].wait()
-    one_block(csmooth, parent_z, 2, one_smooth.at[1], 54)
-    loads[7].wait()
+    one_block(csmooth.at[parent_y], parent_z, 2, one_smooth.at[1], 54)
+    levels_y = lax.div(size["gy"], 2)
+    beside_y = [lax.rem(parent_y + (levels_y + step), levels_y) for step in (-1, 1)]
+    one_block(csmooth.at[beside_y[0]], parent_z, 2, near_smooth.at[2], 61)
+    one_block(csmooth.at[beside_y[1]], parent_z, 2, near_smooth.at[3], 62)
+    one_block(csmooth.at[parent_y], 1 - parent_z, 2, near_smooth.at[4], 63)
+    for side, copy in enumerate(block_copies()):
+        copy.wait_recv()
+    for side in range(2):
+        block = block_recv[side]
+        near_smooth[side] = double(weave(woven.at[59 + side], block, block))
+    loads[12].wait()
+    loads[13].wait()
     one_operator(
         cblocks,
         parent_z,
@@ -520,20 +585,34 @@
     mid_resid = mid_resid - one_apply(0, copies, 1, second)
 
     own = pack(matmul(one_prolong[1], tall(mid_resid)))
-    sib_send[...] = own
-    copies = sib_copies()
-    for copy in copies:
+    term_send[...] = own
+    terms = term_copies()
+    for copy in terms:
         copy.start()
     coarse_inverse, coarse_steps = coefficients(2)
-    for copy in copies:
+    for copy in terms:
         copy.wait_recv()
-    coarse_resid = unpack((own + sib_recv[0]) + (sib_recv[1] + sib_recv[2]))
+
+    def total(m):
+        first = own if m == 0 else term_recv[4 * m]
+        return unpack(
+            (first + term_recv[4 * m + 1]) + (term_recv[4 * m + 2] + term_recv[4 * m + 3])
+        )
+
+    coarse_resid = total(0)
     step = one_smoothed(1, coarse_resid) * coarse_inverse
+    parts = [
+        wide(matmul(near_smooth[m - 1], tall(total(m))) * coarse_inverse) for m in range(1, 6)
+    ]
     coarse_field = step
     for sweep in range(3):
-        copies = coarse_copies(2 + sweep)
-        send_node(2 + sweep, copies, step)
-        coarse_resid = coarse_resid - one_apply(1, copies, 2 + sweep, step)
+        if sweep == 0:
+            change = matmul(one_centre[1], tall(step)) + one_outside(1, parts)
+        else:
+            copies = coarse_copies(2 + sweep)
+            send_node(2 + sweep, copies, step)
+            change = one_apply(1, copies, 2 + sweep, step)
+        coarse_resid = coarse_resid - change
         keep, push = coarse_steps[sweep]
         step = step * keep + one_smoothed(1, coarse_resid) * push
         coarse_field = coarse_field + step
@@ -582,10 +661,10 @@
     for slot in (0, 1, 5, 6):
         for copy in middle_copies(slot):
             copy.wait_send()
-    for slot in (2, 3, 4):
+    for slot in (3, 4):
         for copy in coarse_copies(slot):
             copy.wait_send()
-    for copy in sib_copies():
+    for copy in term_copies() + block_copies():
         copy.wait_send()
 
 
@@ -609,33 +688,18 @@
     csmooth = interleaved(csmooth)[0]
     clinks = jnp.transpose(clinks, (0, 3, 2, 1))
     anywhere = pl.BlockSpec(memory_space=pl.ANY)
-    scalars = pl.BlockSpec(memory_space=pltpu.SMEM)
-    vmem = pl.BlockSpec(memory_space=pltpu.VMEM)
     dma = pltpu.SemaphoreType.DMA
     outs = pl.pallas_call(
         kernel,
-        out_shape=(
-            jax.ShapeDtypeStruct(rhs.shape, F32),
-            jax.ShapeDtypeStruct(rhs.shape, F32),
-        ),
-        in_specs=[
-            anywhere,
-            anywhere,
-            scalars,
-            anywhere,
-            anywhere,
-            anywhere,
-            scalars,
-            anywhere,
-            anywhere,
-            anywhere,
-            scalars,
-            anywhere,
-            scalars,
-            scalars,
-        ],
-        out_specs=(vmem, vmem),
+        out_shape=(pltpu.VMEM(rhs.shape, F32), pltpu.VMEM(rhs.shape, F32)),
+        in_specs=[anywhere] * 14,
+        out_specs=(pl.BlockSpec(memory_space=pltpu.VMEM),) * 2,
         scratch_shapes=[
+            pltpu.SMEM(flinks.shape, jnp.int32),
+            pltpu.SMEM(mlinks.shape, jnp.int32),
+            pltpu.SMEM(clinks.shape, jnp.int32),
+            pltpu.SMEM(lowers.shape, F32),
+            pltpu.SMEM(uppers.shape, F32),
             pltpu.VMEM(rhs.shape, F32),
             pltpu.VMEM(fblocks.shape, F32),
             pltpu.VMEM(fsmooth.shape, F32),
@@ -644,10 +708,10 @@
             pltpu.VMEM(msmooth.shape, F32),
             pltpu.VMEM(mprolong.shape, F32),
             pltpu.VMEM(cblocks.shape[1:], F32),
-            pltpu.VMEM(csmooth.shape[1:], F32),
-            dma((9,)),
+            pltpu.VMEM(csmooth.shape, F32),
+            dma((14,)),
             pltpu.VMEM((2, 64, 128), F32),
-            pltpu.VMEM((59, 64, 128), F32),
+            pltpu.VMEM((64, 64, 128), F32),
             pltpu.VMEM((2, 512, 256), BF16),
             pltpu.VMEM((2, 512, 256), BF16),
             pltpu.VMEM((2, 256, 256), BF16),
@@ -663,13 +727,18 @@
             pltpu.VMEM((7, 16, 128), F32),
             pltpu.VMEM((7, 6, 16, 128), F32),
             pltpu.VMEM((16, 128), F32),
-            pltpu.VMEM((3, 16, 128), F32),
+            pltpu.VMEM((24, 16, 128), F32),
+            pltpu.VMEM((32, 128), F32),
+            pltpu.VMEM((2, 32, 128), F32),
+            pltpu.VMEM((5, 64, 256), BF16),
             dma((5, 6)),
             dma((5, 6)),
             dma((7, 6)),
             dma((7, 6)),
-            dma((3,)),
-            dma((3,)),
+            dma((24,)),
+            dma((24,)),
+            dma((2,)),
+            dma((2,)),
         ],
         compiler_params=pltpu.CompilerParams(
             collective_id=0, has_side_effects=True, vmem_limit_bytes=56 * 1024 * 1024

time: 84.3 us -> 80 us (0.949)
  Pallas kernels: 80.4 us -> 78 us
  local copies, waits for them, and re-layouts: 2.95 us -> 1.26 us
    pallas_call x1, Pallas kernels: 80.4 us -> 78 us  [body(): pl.pallas_call(kernel, out_shape=(pltpu.VMEM(rhs.shape, F32), pltpu.VMEM(...]
    unnamed x2, local copies, waits for them, and re-layouts: 2.95 us -> 1.26 us
where the time goes in v1:
time: 80 us; the launch traced here: 79.9 us
  Pallas kernels  78 us (98%)
  local copies, waits for them, and re-layouts  1.26 us (2%)
    pallas_call x1, Pallas kernels, body(): pl.pallas_call(kernel, out_shape=(pltpu.VMEM(rhs.shape, F32), pltpu.VMEM(...  78 us

profile of v1, /device:TPU:1, one launch (start us, length us, event | category | flops | bytes accessed | tf_op | source)
XLA Modules:
  0.0 79.9 jit_solution(1712832507662911322)
XLA Ops:
  0.6 78.0 %shard_map.149 = (f32[2,2,32,128]{3,2,1,0:T(8,128)S(1)}, f32[2,2,32,128]{3,2,1,0:T(8,128)S(1)}) custom-call(f32[2,2,32,128]{3,2,1,0:T(8,128)} %bitcast.70, f32[2,2,7,64,128]{4,3,2,1,0:T(8,128)} %bitcast.65, s32[2,2,2,6]{3,2,1,0:T(2,128)} %flinks_hbm.1, f32[2,2,64,128]{3,2,1,0:T(8,128)} %bitcast.68, f32[2,2,64,128]{3,2,1,0:T(8,128)} %bitcast.69, ...), custom_call_target="tpu_custom_call" | custom-call | tf_op jit(solution)/shard_map/pallas_call | solution.py:692
  78.6 0.6 copy.29
  79.3 0.6 copy.30
